TPU v7x, 32 devices: a whole 2x2x4 slice. The times are simulated.
32 devices in a mesh: seq: 8 (over z, x), dp: 4 (over y, core).
Axes of the slice: x: 2, y: 2, z: 4, core: 2. Of those that a mesh axis runs over, the one named last changes fastest.
Arguments:
- signal: bfloat16 [16384, 128], P(('seq', 'dp')), may hold values from -6 to 6
- filter_param: bfloat16 [16384, 128], P(('seq', 'dp')), may hold values from -6 to 6
- skip_gain: float32 [128], replicated, may hold values from 0.5 to 1.5
- out_grad: bfloat16 [16384, 128], P(('seq', 'dp')), may hold values from -6 to 6
Outputs:
- conv_out: bfloat16 [16384, 128], P(('seq', 'dp'))
- input_grad: bfloat16 [16384, 128], P(('seq', 'dp'))
- filter_grad: float32 [16384, 128], P(('seq', 'dp'))
All inputs are finite; a program needn't handle non-finite values.
Results may differ from a plain program's by a relative error of at most 0.001.
Values may be sent and summed in bfloat16 or wider, within the bound.
A program may use at most 64 MiB of HBM per device.

v0:
```python
import math

import jax
import jax.numpy as jnp
from jax import lax
from jax.sharding import PartitionSpec as P

FIRST_LEN = 512


highest = lax.Precision.HIGHEST


def tables(order):
    counter = jnp.arange(order, dtype=jnp.int32)
    product = counter[:, None] * counter[None, :] % order
    angle = product.astype(jnp.float32) * (2.0 * math.pi / order)
    return (jnp.cos(angle), jnp.sin(angle))


def forward_spec(stacked, dev_count, first_len):
    tok_rows, chans = stacked.shape
    first_dev = first_len // dev_count
    second_len = tok_rows // first_dev
    second_dev = second_len // dev_count
    length = first_len * second_len
    blocks = stacked.reshape(first_dev, second_len, chans)
    columns = lax.all_to_all(blocks, ("seq", "dp"), split_axis=1, concat_axis=0, tiled=True)
    cos_a, sin_a = tables(first_len)
    flat = columns.astype(jnp.float32).reshape(first_len, second_dev * chans)
    real_part = jnp.dot(cos_a, flat, precision=highest).reshape(first_len, second_dev, chans)
    imag_part = -jnp.dot(sin_a, flat, precision=highest).reshape(first_len, second_dev, chans)
    freq_idx = jnp.arange(first_len, dtype=jnp.int32)
    pos_idx = lax.axis_index(("seq", "dp")) * second_dev + jnp.arange(second_dev, dtype=jnp.int32)
    phase = (freq_idx[:, None] * pos_idx[None, :] % length).astype(jnp.float32)
    phase = (phase * (-2.0 * math.pi / length))[:, :, None]
    tw_cos = jnp.cos(phase)
    tw_sin = jnp.sin(phase)
    rot_re = real_part * tw_cos - imag_part * tw_sin
    rot_im = real_part * tw_sin + imag_part * tw_cos
    spec_re, spec_im = (
        lax.all_to_all(rot_re, ("seq", "dp"), split_axis=0, concat_axis=1, tiled=True),
        lax.all_to_all(rot_im, ("seq", "dp"), split_axis=0, concat_axis=1, tiled=True),
    )
    cos_b, sin_b = tables(second_len)
    out_re = jnp.einsum("qbc,bk->qkc", spec_re, cos_b, precision=highest) + jnp.einsum(
        "qbc,bk->qkc", spec_im, sin_b, precision=highest
    )
    out_im = jnp.einsum("qbc,bk->qkc", spec_im, cos_b, precision=highest) - jnp.einsum(
        "qbc,bk->qkc", spec_re, sin_b, precision=highest
    )
    return (columns, out_re, out_im)


def inverse_time(spec_re, spec_im, dev_count, first_len):
    first_dev, second_len, chans = spec_re.shape
    second_dev = second_len // dev_count
    length = first_len * second_len
    cos_b, sin_b = tables(second_len)
    unit_re = jnp.einsum("qkc,kb->qbc", spec_re, cos_b, precision=highest) - jnp.einsum(
        "qkc,kb->qbc", spec_im, sin_b, precision=highest
    )
    unit_im = jnp.einsum("qkc,kb->qbc", spec_im, cos_b, precision=highest) + jnp.einsum(
        "qkc,kb->qbc", spec_re, sin_b, precision=highest
    )
    freq_idx = lax.axis_index(("seq", "dp")) * first_dev + jnp.arange(first_dev, dtype=jnp.int32)
    pos_idx = jnp.arange(second_len, dtype=jnp.int32)
    phase = (freq_idx[:, None] * pos_idx[None, :] % length).astype(jnp.float32)
    phase = (phase * (2.0 * math.pi / length))[:, :, None]
    tw_cos = jnp.cos(phase)
    tw_sin = jnp.sin(phase)
    rot_re = unit_re * tw_cos - unit_im * tw_sin
    rot_im = unit_re * tw_sin + unit_im * tw_cos
    col_re, col_im = (
        lax.all_to_all(rot_re, ("seq", "dp"), split_axis=1, concat_axis=0, tiled=True),
        lax.all_to_all(rot_im, ("seq", "dp"), split_axis=1, concat_axis=0, tiled=True),
    )
    cos_a, sin_a = tables(first_len)
    flat_re = col_re.reshape(first_len, second_dev * chans)
    flat_im = col_im.reshape(first_len, second_dev * chans)
    values = jnp.dot(cos_a, flat_re, precision=highest) - jnp.dot(sin_a, flat_im, precision=highest)
    return (values * (1.0 / length)).reshape(first_len, second_dev, chans)


def per_device(signal, filter_param, skip_gain, out_grad):
    dev_count = lax.axis_size(("seq", "dp"))
    chans = skip_gain.shape[0]
    tok_rows = filter_param.shape[0]
    length = tok_rows * dev_count
    scale = 1.0 / math.sqrt(length)
    stacked = jnp.concatenate([signal, out_grad, filter_param], axis=1)
    columns, spec_re, spec_im = forward_spec(stacked, dev_count, FIRST_LEN)
    sig_re = spec_re[:, :, :chans]
    sig_im = spec_im[:, :, :chans]
    cot_re = spec_re[:, :, chans : 2 * chans]
    cot_im = spec_im[:, :, chans : 2 * chans]
    filt_re = spec_re[:, :, 2 * chans :] * scale
    filt_im = spec_im[:, :, 2 * chans :] * scale
    conv_re = sig_re * filt_re - sig_im * filt_im
    conv_im = sig_re * filt_im + sig_im * filt_re
    back_re = filt_re * cot_re + filt_im * cot_im
    back_im = filt_re * cot_im - filt_im * cot_re
    taps_re = sig_re * cot_re + sig_im * cot_im
    taps_im = sig_re * cot_im - sig_im * cot_re
    joined_re = jnp.concatenate([conv_re, back_re, taps_re], axis=2)
    joined_im = jnp.concatenate([conv_im, back_im, taps_im], axis=2)
    times = inverse_time(joined_re, joined_im, dev_count, FIRST_LEN)
    conv_cols = (
        times[:, :, :chans] + skip_gain * columns[:, :, :chans].astype(jnp.float32)
    ).astype(jnp.bfloat16)
    back_cols = (
        times[:, :, chans : 2 * chans]
        + skip_gain * columns[:, :, chans : 2 * chans].astype(jnp.float32)
    ).astype(jnp.bfloat16)
    both_rows = lax.all_to_all(
        jnp.concatenate([conv_cols, back_cols], axis=2),
        ("seq", "dp"),
        split_axis=0,
        concat_axis=1,
        tiled=True,
    )
    both_rows = both_rows.reshape(tok_rows, 2 * chans)
    conv_out = both_rows[:, :chans]
    input_grad = both_rows[:, chans:]
    taps_cols = times[:, :, 2 * chans :] * scale
    taps_rows = lax.all_to_all(taps_cols, ("seq", "dp"), split_axis=0, concat_axis=1, tiled=True)
    filter_grad = taps_rows.reshape(tok_rows, chans)
    return (conv_out, input_grad, filter_grad)


def solution(mesh):
    placed = (P(("seq", "dp"), None), P(("seq", "dp"), None), P(), P(("seq", "dp"), None))
    return jax.shard_map(
        per_device,
        mesh=mesh,
        in_specs=placed,
        out_specs=(P(("seq", "dp"), None), P(("seq", "dp"), None), P(("seq", "dp"), None)),
        check_vma=False,
    )
```

profile of v0, /device:TPU:0, one launch (start us, length us, event | category | flops | bytes accessed | tf_op | source)
XLA Modules:
  0.0 178.2 jit_solution(17987065417323165292)
XLA Ops:
  0.6 1.1 pad_maximum_fusion.6
  1.7 0.9 copy.43
  2.6 7.3 %all-to-all-start = ((bf16[16,32,384]{2,0,1:T(8,128)(2,1)}), bf16[16,32,384]{2,0,1:T(8,128)(2,1)S(1)}, u32[]{:S(2)}, u32[]{:S(2)}) async-start(bf16[16,32,384]{2,0,1:T(8,128)(2,1)} %copy.43), calls=%async_computation | async-start | bytes 786432 | tf_op jit(solution)/shard_map/all_to_all | solution.py:28
  9.9 0.1 fusion.69
  10.0 13.1 %all-to-all-done = bf16[16,32,384]{2,0,1:T(8,128)(2,1)S(1)} async-done(((bf16[16,32,384]{2,0,1:T(8,128)(2,1)}), bf16[16,32,384]{2,0,1:T(8,128)(2,1)S(1)}, u32[]{:S(2)}, u32[]{:S(2)}) %all-to-all-start) | async-done | bytes 393248 | tf_op jit(solution)/shard_map/all_to_all | solution.py:28
  23.1 5.4 %convolution_negate_fusion = f32[512,384]{1,0:T(8,128)S(1)} fusion(bf16[512,384]{1,0:T(8,128)(2,1)S(1)} %bitcast.85), kind=kOutput, calls=%fused_computation.12 | convolution fusion | flops 1211826176 | bytes 1179648 | tf_op jit(solution)/shard_map/dot_general | solution.py:32
  28.5 6.4 %subtract_bitcast_fusion = (f32[512,1,384]{2,0,1:T(8,128)S(1)}, f32[512,1,384]{2,0,1:T(8,128)S(1)}) fusion(f32[512,384]{1,0:T(8,128)S(1)} %convolution_negate_fusion, f32[512]{0:T(512)S(1)} %get-tuple-element.22, f32[512]{0:T(512)S(1)} %get-tuple-element.23, bf16[512,384]{1,0:T(8,128)(2,1)S(1)} %bitcast.86), kind=kOutput, calls=%fused_computation.32 | convolution fusion | flops 1212809216 | bytes 2756608 | tf_op jit(solution)/shard_map/dot_general | solution.py:31
  34.8 1.7 copy.44
  36.6 2.6 %all-to-all-start.1 = ((f32[512,1,384]{2,1,0:T(1,128)}), f32[512,1,384]{2,1,0:T(1,128)S(1)}, u32[]{:S(2)}, u32[]{:S(2)}) async-start(f32[512,1,384]{2,1,0:T(1,128)} %copy.44), calls=%async_computation.1 | async-start | bytes 1572864 | tf_op jit(solution)/shard_map/all_to_all | solution.py:42
  39.2 1.7 copy.46
  40.9 18.9 %all-to-all-done.1 = f32[512,1,384]{2,1,0:T(1,128)S(1)} async-done(((f32[512,1,384]{2,1,0:T(1,128)}), f32[512,1,384]{2,1,0:T(1,128)S(1)}, u32[]{:S(2)}, u32[]{:S(2)}) %all-to-all-start.1) | async-done | bytes 786464 | tf_op jit(solution)/shard_map/all_to_all | solution.py:42
  59.8 3.8 %all-to-all-start.2 = ((f32[512,1,384]{2,1,0:T(1,128)}), f32[512,1,384]{2,1,0:T(1,128)S(1)}, u32[]{:S(2)}, u32[]{:S(2)}) async-start(f32[512,1,384]{2,1,0:T(1,128)} %copy.46), calls=%async_computation.2 | async-start | bytes 1572864 | tf_op jit(solution)/shard_map/all_to_all | solution.py:43
  63.6 0.1 fusion.65
  63.8 0.1 copy.56
  63.8 1.0 fusion.13
  64.9 19.2 %all-to-all-done.2 = f32[512,1,384]{2,1,0:T(1,128)S(1)} async-done(((f32[512,1,384]{2,1,0:T(1,128)}), f32[512,1,384]{2,1,0:T(1,128)S(1)}, u32[]{:S(2)}, u32[]{:S(2)}) %all-to-all-start.2) | async-done | bytes 786464 | tf_op jit(solution)/shard_map/all_to_all | solution.py:43
  84.1 0.1 copy.57
  84.1 1.0 fusion.15
  85.1 1.0 fusion.3
  86.2 1.0 fusion.2
  87.2 0.1 multiply_add_fusion.3
  87.3 0.2 multiply_subtract_fusion.3
  87.4 0.9 fusion.23
  88.3 0.9 fusion.22
  89.2 0.9 fusion.1
  90.0 1.0 multiply_add_fusion
  91.1 1.3 copy.48
  92.4 3.6 %all-to-all-start.3 = ((f32[16,32,384]{2,0,1:T(8,128)}), f32[16,32,384]{2,0,1:T(8,128)S(1)}, u32[]{:S(2)}, u32[]{:S(2)}) async-start(f32[16,32,384]{2,0,1:T(8,128)} %copy.48), calls=%async_computation.3 | async-start | bytes 1572864 | tf_op jit(solution)/shard_map/all_to_all | solution.py:75
  96.1 1.4 copy.49
  97.4 19.2 %all-to-all-done.3 = f32[16,32,384]{2,0,1:T(8,128)S(1)} async-done(((f32[16,32,384]{2,0,1:T(8,128)}), f32[16,32,384]{2,0,1:T(8,128)S(1)}, u32[]{:S(2)}, u32[]{:S(2)}) %all-to-all-start.3) | async-done | bytes 786464 | tf_op jit(solution)/shard_map/all_to_all | solution.py:75
  116.7 3.8 %all-to-all-start.4 = ((f32[16,32,384]{2,0,1:T(8,128)}), f32[16,32,384]{2,0,1:T(8,128)S(1)}, u32[]{:S(2)}, u32[]{:S(2)}) async-start(f32[16,32,384]{2,0,1:T(8,128)} %copy.49), calls=%async_computation.4 | async-start | bytes 1572864 | tf_op jit(solution)/shard_map/all_to_all | solution.py:76
  120.6 0.1 copy.59
  120.7 0.1 copy.60
  120.8 6.6 %fusion.26 = f32[512,384]{0,1:T(8,128)S(1)} fusion(f32[512,384]{1,0:T(8,128)S(1)} %bitcast.91), kind=kOutput, calls=%fused_computation.41 | convolution fusion | flops 1211629568 | bytes 1572864 | tf_op jit(solution)/shard_map/dot_general | solution.py:81
  127.4 13.5 %all-to-all-done.4 = f32[16,32,384]{2,0,1:T(8,128)S(1)} async-done(((f32[16,32,384]{2,0,1:T(8,128)}), f32[16,32,384]{2,0,1:T(8,128)S(1)}, u32[]{:S(2)}, u32[]{:S(2)}) %all-to-all-start.4) | async-done | bytes 786464 | tf_op jit(solution)/shard_map/all_to_all | solution.py:76
  140.9 0.0 copy-start
  140.9 6.7 %fusion.5 = f32[512,1,384]{0,2,1:T(8,128)S(1)} fusion(f32[512,384]{0,1:T(8,128)S(1)} %fusion.26, f32[512,384]{1,0:T(8,128)S(1)} %bitcast.92), kind=kOutput, calls=%fused_computation.14 | convolution fusion | flops 1212022784 | bytes 2359296 | tf_op jit(solution)/shard_map/dot_general | solution.py:81
  147.6 0.0 copy-done
  147.6 0.1 fusion.33
  147.8 0.5 broadcast.290
  148.3 0.8 reduce
  149.1 0.1 copy.77
  149.2 0.8 reshape.156
  150.0 3.6 %all-to-all-start.5 = ((bf16[32,2,2048]{2,1,0:T(2,128)(2,1)}), bf16[32,2,2048]{2,1,0:T(2,128)(2,1)S(1)}, u32[]{:S(2)}, u32[]{:S(2)}) async-start(bf16[32,2,2048]{2,1,0:T(2,128)(2,1)} %reshape.156), calls=%async_computation.5 | async-start | bytes 524288 | tf_op jit(solution)/shard_map/all_to_all | solution.py:115
  153.6 0.8 copy.54
  154.5 9.8 %all-to-all-done.5 = bf16[32,2,2048]{2,1,0:T(2,128)(2,1)S(1)} async-done(((bf16[32,2,2048]{2,1,0:T(2,128)(2,1)}), bf16[32,2,2048]{2,1,0:T(2,128)(2,1)S(1)}, u32[]{:S(2)}, u32[]{:S(2)}) %all-to-all-start.5) | async-done | bytes 262176 | tf_op jit(solution)/shard_map/all_to_all | solution.py:115
  164.2 2.6 %all-to-all-start.6 = ((f32[512,1,128]{2,1,0:T(1,128)}), f32[512,1,128]{2,1,0:T(1,128)S(1)}, u32[]{:S(2)}, u32[]{:S(2)}) async-start(f32[512,1,128]{2,1,0:T(1,128)} %copy.54), calls=%async_computation.6 | async-start | bytes 524288 | tf_op jit(solution)/shard_map/all_to_all | solution.py:126
  166.8 0.3 reshape.157
  167.2 0.1 copy.53
  167.2 0.7 fusion.124
  168.0 9.5 %all-to-all-done.6 = f32[512,1,128]{2,1,0:T(1,128)S(1)} async-done(((f32[512,1,128]{2,1,0:T(1,128)}), f32[512,1,128]{2,1,0:T(1,128)S(1)}, u32[]{:S(2)}, u32[]{:S(2)}) %all-to-all-start.6) | async-done | bytes 262176 | tf_op jit(solution)/shard_map/all_to_all | solution.py:126
  177.4 0.8 copy.55
  (4 shorter events, 0.1 us)
Async XLA Ops:
  2.6 20.5 %all-to-all-start = ((bf16[16,32,384]{2,0,1:T(8,128)(2,1)}), bf16[16,32,384]{2,0,1:T(8,128)(2,1)S(1)}, u32[]{:S(2)}, u32[]{:S(2)}) async-start(bf16[16,32,384]{2,0,1:T(8,128)(2,1)} %copy.43), calls=%async_computation | async-start | bytes 786432 | tf_op jit(solution)/shard_map/all_to_all | solution.py:28
  36.6 23.3 %all-to-all-start.1 = ((f32[512,1,384]{2,1,0:T(1,128)}), f32[512,1,384]{2,1,0:T(1,128)S(1)}, u32[]{:S(2)}, u32[]{:S(2)}) async-start(f32[512,1,384]{2,1,0:T(1,128)} %copy.44), calls=%async_computation.1 | async-start | bytes 1572864 | tf_op jit(solution)/shard_map/all_to_all | solution.py:42
  59.8 24.2 %all-to-all-start.2 = ((f32[512,1,384]{2,1,0:T(1,128)}), f32[512,1,384]{2,1,0:T(1,128)S(1)}, u32[]{:S(2)}, u32[]{:S(2)}) async-start(f32[512,1,384]{2,1,0:T(1,128)} %copy.46), calls=%async_computation.2 | async-start | bytes 1572864 | tf_op jit(solution)/shard_map/all_to_all | solution.py:43
  92.4 24.3 %all-to-all-start.3 = ((f32[16,32,384]{2,0,1:T(8,128)}), f32[16,32,384]{2,0,1:T(8,128)S(1)}, u32[]{:S(2)}, u32[]{:S(2)}) async-start(f32[16,32,384]{2,0,1:T(8,128)} %copy.48), calls=%async_computation.3 | async-start | bytes 1572864 | tf_op jit(solution)/shard_map/all_to_all | solution.py:75
  116.7 24.2 %all-to-all-start.4 = ((f32[16,32,384]{2,0,1:T(8,128)}), f32[16,32,384]{2,0,1:T(8,128)S(1)}, u32[]{:S(2)}, u32[]{:S(2)}) async-start(f32[16,32,384]{2,0,1:T(8,128)} %copy.49), calls=%async_computation.4 | async-start | bytes 1572864 | tf_op jit(solution)/shard_map/all_to_all | solution.py:76
  140.9 6.7 %copy-start = (f32[128]{0:T(128)S(1)}, f32[128]{0:T(128)}, u32[]{:S(2)}) copy-start(f32[128]{0:T(128)} %param.6) | copy-start | bytes 1540
  150.0 14.2 %all-to-all-start.5 = ((bf16[32,2,2048]{2,1,0:T(2,128)(2,1)}), bf16[32,2,2048]{2,1,0:T(2,128)(2,1)S(1)}, u32[]{:S(2)}, u32[]{:S(2)}) async-start(bf16[32,2,2048]{2,1,0:T(2,128)(2,1)} %reshape.156), calls=%async_computation.5 | async-start | bytes 524288 | tf_op jit(solution)/shard_map/all_to_all | solution.py:115
  164.2 13.2 %all-to-all-start.6 = ((f32[512,1,128]{2,1,0:T(1,128)}), f32[512,1,128]{2,1,0:T(1,128)S(1)}, u32[]{:S(2)}, u32[]{:S(2)}) async-start(f32[512,1,128]{2,1,0:T(1,128)} %copy.54), calls=%async_computation.6 | async-start | bytes 524288 | tf_op jit(solution)/shard_map/all_to_all | solution.py:126
where the time goes:
time: 179 us; the launch traced here: 178 us
  waiting for transfers between devices  103 us (58%)
  matrix products  32.7 us (18%)
  starting transfers between devices  27.4 us (15%)
  local copies, waits for them, and re-layouts  11.5 us (6%)
  other arithmetic  2.46 us (1%)
    all_to_all x1, waiting for transfers between devices, inverse_time(): lax.all_to_all(rot_re, ('seq', 'dp'), split_axis=1, concat_axis=0, tiled=...  19.2 us
    all_to_all x1, waiting for transfers between devices, forward_spec(): lax.all_to_all(rot_im, ('seq', 'dp'), split_axis=0, concat_axis=1, tiled=...  19.2 us
    all_to_all x1, waiting for transfers between devices, forward_spec(): lax.all_to_all(rot_re, ('seq', 'dp'), split_axis=0, concat_axis=1, tiled=...  18.9 us
    all_to_all x1, waiting for transfers between devices, inverse_time(): lax.all_to_all(rot_im, ('seq', 'dp'), split_axis=1, concat_axis=0, tiled=...  13.5 us
    all_to_all x1, waiting for transfers between devices, forward_spec(): lax.all_to_all(blocks, ('seq', 'dp'), split_axis=1, concat_axis=0, tiled=...  13.1 us
    all_to_all x1, waiting for transfers between devices, per_device(): lax.all_to_all(jnp.concatenate([conv_cols, back_cols], axis=2), ('seq', '...  9.77 us
    all_to_all x1, waiting for transfers between devices, per_device(): lax.all_to_all(taps_cols, ('seq', 'dp'), split_axis=0, concat_axis=1, til...  9.45 us
    all_to_all x1, starting transfers between devices, forward_spec(): lax.all_to_all(blocks, ('seq', 'dp'), split_axis=1, concat_axis=0, tiled=...  7.3 us
  transfers between devices with their start and end apart: 7, of which 7 were waited for; matrix products, arithmetic and copies ran while one was open for 7% of the time, Pallas kernels for 0%

commit v1 on v0

v1 whole, which is shorter than its diff:
```python
import functools
import math

import jax
import jax.numpy as jnp
import ml_dtypes
import numpy as np
from jax import lax
from jax.experimental import pallas as pl
from jax.experimental.pallas import tpu as pltpu
from jax.sharding import PartitionSpec as P

LANES = 128
MESH = pl.DeviceIdType.MESH


def round_up(value, step):
    return -(-value // step) * step


def split_table(table):
    high = table.astype(np.float32).astype(ml_dtypes.bfloat16)
    low = (table - high.astype(np.float64)).astype(np.float32).astype(ml_dtypes.bfloat16)
    return high, low


def make_tables(length, sources):
    outer = length // LANES
    runs = outer // sources
    half = round_up(outer // 2 + 1, 16)
    k1 = np.arange(half)
    a = (np.arange(sources)[None, :] * runs + np.arange(runs)[:, None]).reshape(-1)
    kept = (k1 <= outer // 2).astype(np.float64)
    angle = 2.0 * math.pi * ((k1[:, None] * a[None, :]) % outer) / outer
    left = np.concatenate([np.cos(angle) * kept[:, None], -np.sin(angle) * kept[:, None]], axis=0)
    left = np.concatenate(split_table(left), axis=1)
    b = np.arange(LANES)
    turn = 2.0 * math.pi * ((k1[:, None] * b[None, :]) % length) / length
    twiddle = np.stack([np.cos(turn), -np.sin(turn)]).astype(np.float32)
    inner = 2.0 * math.pi * ((b[:, None] * b[None, :]) % LANES) / LANES
    cos, sin = np.cos(inner), np.sin(inner)
    right = np.stack(split_table(np.block([[cos, -sin], [sin, cos]])))
    right_inv = np.stack(split_table(np.block([[cos, sin], [-sin, cos]])))
    weight = kept * np.where((k1 == 0) | (2 * k1 == outer), 1.0, 2.0) / length
    left_inv = np.concatenate([np.cos(angle) * weight[:, None], -np.sin(angle) * weight[:, None]], axis=0).T
    high, low = split_table(left_inv)
    left_inv = np.concatenate([high, high, low], axis=1)
    return left, twiddle, right, right_inv, left_inv


def split(value):
    high = value.astype(jnp.bfloat16)
    low = (value - high.astype(jnp.float32)).astype(jnp.bfloat16)
    return high, low


def dot(a, b):
    return jnp.dot(a, b, preferred_element_type=jnp.float32)


def right_product(value, table_ref):
    high, low = split(value)
    return dot(high, table_ref[0]) + dot(low, table_ref[0]) + dot(high, table_ref[1])


def kernel(
    devs, inner_devs, scale,
    gain_ref, sig_ref, filt_ref, cot_ref,
    left_hbm, twiddle_hbm, right_hbm, right_inv_hbm, left_inv_hbm,
    conv_ref, back_ref, taps_ref,
    left_ref, twiddle_ref, right_ref, right_inv_ref, left_inv_ref,
    wide_in, send_in, recv_in, wide_out, send_out, recv_out, send_taps, recv_taps,
    table_sem, own_sem, send_sem, recv_sem,
):
    rows, chans = sig_ref.shape
    runs = rows // LANES
    mine = chans // devs
    outer = runs * devs
    half = twiddle_ref.shape[1]
    rows_in = send_in.shape[1]
    rows_out = send_out.shape[1]
    rows_taps = send_taps.shape[1]
    me = lax.axis_index("seq") * inner_devs + lax.axis_index("dp")

    def place(index):
        return (index // inner_devs, lax.rem(index, inner_devs))

    barrier = pltpu.get_barrier_semaphore()

    def greet(step, carry):
        pl.semaphore_signal(barrier, inc=1, device_id=place(lax.rem(me + step, devs)), device_id_type=MESH)
        return carry

    lax.fori_loop(1, devs, greet, 0)

    tables = [
        pltpu.make_async_copy(src, dst, table_sem.at[at])
        for at, (src, dst) in enumerate(
            [
                (left_hbm, left_ref),
                (twiddle_hbm, twiddle_ref),
                (right_hbm, right_ref),
                (right_inv_hbm, right_inv_ref),
                (left_inv_hbm, left_inv_ref),
            ]
        )
    ]
    for copy in tables:
        copy.start()

    for at, ref in enumerate((sig_ref, cot_ref, filt_ref)):
        for run in range(runs):
            block = ref[run * LANES : (run + 1) * LANES, :].astype(jnp.float32).T
            for c in range(mine):
                wide_in[pl.ds((at * mine + c) * runs + run, devs, stride=rows_in), :] = block[
                    c * devs : (c + 1) * devs, :
                ]
    send_in[...] = wide_in[...].astype(jnp.bfloat16).reshape(devs, rows_in, LANES)

    pl.semaphore_wait(barrier, devs - 1)

    def exchange(kind, send, recv):
        own = pltpu.make_async_copy(send.at[me], recv.at[me], own_sem.at[kind])
        own.start()

        def remote(to, slot_from, slot_send):
            return pltpu.make_async_remote_copy(
                src_ref=send.at[to],
                dst_ref=recv.at[slot_from],
                send_sem=send_sem.at[kind, slot_send],
                recv_sem=recv_sem.at[kind, slot_from],
                device_id=place(to),
                device_id_type=MESH,
            )

        def begin(step, carry):
            to = lax.rem(me + step, devs)
            remote(to, me, to).start()
            return carry

        lax.fori_loop(1, devs, begin, 0)

        def finish():
            own.wait()

            def arrive(step, carry):
                other = lax.rem(me + devs - step, devs)
                remote(other, other, other).wait_recv()
                return carry

            lax.fori_loop(1, devs, arrive, 0)

        def drain():
            def left_device(step, carry):
                to = lax.rem(me + step, devs)
                remote(to, me, to).wait_send()
                return carry

            lax.fori_loop(1, devs, left_device, 0)

        return finish, drain

    finish_in, drain_in = exchange(0, send_in, recv_in)
    for copy in tables:
        copy.wait()
    finish_in()
    wide_in[...] = recv_in[...].astype(jnp.float32).reshape(devs * rows_in, LANES)

    def column(at, c):
        return jnp.concatenate(
            [wide_in[pl.ds((at * mine + c) * runs + run, devs, stride=rows_in), :] for run in range(runs)],
            axis=0,
        )

    tw_re, tw_im = twiddle_ref[0], twiddle_ref[1]
    columns = [[column(at, c) for c in range(mine)] for at in range(3)]
    spectra = []
    for at in range(3):
        flat = jnp.concatenate(columns[at], axis=1).astype(jnp.bfloat16)
        partial = dot(left_ref[...], jnp.concatenate([flat, flat], axis=0))
        turned = []
        for c in range(mine):
            re = partial[:half, c * LANES : (c + 1) * LANES]
            im = partial[half:, c * LANES : (c + 1) * LANES]
            turned.append(jnp.concatenate([re * tw_re - im * tw_im, re * tw_im + im * tw_re], axis=1))
        spec = right_product(jnp.concatenate(turned, axis=0), right_ref)
        spectra.append((spec[:, :LANES], spec[:, LANES:]))
    (sig_re, sig_im), (cot_re, cot_im), (filt_re, filt_im) = spectra
    filt_re, filt_im = filt_re * scale, filt_im * scale

    def inverse(re, im):
        unit = right_product(jnp.concatenate([re, im], axis=1), right_inv_ref)
        turned = []
        for c in range(mine):
            u_re = unit[c * half : (c + 1) * half, :LANES]
            u_im = unit[c * half : (c + 1) * half, LANES:]
            turned.append(jnp.concatenate([u_re * tw_re + u_im * tw_im, u_im * tw_re - u_re * tw_im], axis=0))
        high, low = split(jnp.concatenate(turned, axis=1))
        return dot(left_inv_ref[...], jnp.concatenate([high, low, high], axis=0))

    taps = inverse(sig_re * cot_re + sig_im * cot_im, sig_re * cot_im - sig_im * cot_re) * scale
    for c in range(mine):
        for run in range(runs):
            send_taps_rows = taps[run * devs : (run + 1) * devs, c * LANES : (c + 1) * LANES]
            wide_out[pl.ds(c * runs + run, devs, stride=rows_taps), :] = send_taps_rows
    send_taps[...] = wide_out[0 : devs * rows_taps, :].reshape(devs, rows_taps, LANES)
    finish_taps, drain_taps = exchange(1, send_taps, recv_taps)

    gains = [gain_ref[c * devs + me] for c in range(mine)]
    conv = inverse(sig_re * filt_re - sig_im * filt_im, sig_re * filt_im + sig_im * filt_re)
    back = inverse(filt_re * cot_re + filt_im * cot_im, filt_re * cot_im - filt_im * cot_re)
    for at, value in enumerate((conv, back)):
        for c in range(mine):
            done = value[:, c * LANES : (c + 1) * LANES] + gains[c] * columns[at][c]
            for run in range(runs):
                wide_out[pl.ds((at * mine + c) * runs + run, devs, stride=rows_out), :] = done[
                    run * devs : (run + 1) * devs, :
                ]
    send_out[...] = wide_out[0 : devs * rows_out, :].astype(jnp.bfloat16).reshape(devs, rows_out, LANES)
    finish_out, drain_out = exchange(2, send_out, recv_out)

    def place_rows(source, at, stride, out_ref):
        for run in range(runs):
            block = jnp.concatenate(
                [source[pl.ds((at * mine + c) * runs + run, devs, stride=stride), :] for c in range(mine)],
                axis=0,
            )
            out_ref[run * LANES : (run + 1) * LANES, :] = block.T.astype(out_ref.dtype)

    finish_taps()
    wide_in[0 : devs * rows_taps, :] = recv_taps[...].reshape(devs * rows_taps, LANES)
    place_rows(wide_in, 0, rows_taps, taps_ref)
    finish_out()
    wide_in[0 : devs * rows_out, :] = recv_out[...].astype(jnp.float32).reshape(devs * rows_out, LANES)
    place_rows(wide_in, 0, rows_out, conv_ref)
    place_rows(wide_in, 1, rows_out, back_ref)
    drain_in()
    drain_taps()
    drain_out()


def per_device(devs, inner_devs, signal, filter_param, skip_gain, out_grad):
    rows, chans = signal.shape
    length = rows * devs
    mine = chans // devs
    runs = rows // LANES
    rows_in = round_up(3 * mine * runs, 16)
    rows_out = round_up(2 * mine * runs, 16)
    rows_taps = round_up(mine * runs, 8)
    tables = [jnp.asarray(table) for table in make_tables(length, devs)]
    bf16, f32 = jnp.bfloat16, jnp.float32
    vmem = pl.BlockSpec(memory_space=pltpu.VMEM)
    return pl.pallas_call(
        functools.partial(kernel, devs, inner_devs, 1.0 / math.sqrt(length)),
        out_shape=(
            jax.ShapeDtypeStruct((rows, chans), bf16),
            jax.ShapeDtypeStruct((rows, chans), bf16),
            jax.ShapeDtypeStruct((rows, chans), f32),
        ),
        in_specs=[pl.BlockSpec(memory_space=pltpu.SMEM)] + [vmem] * 3 + [pl.BlockSpec(memory_space=pl.ANY)] * 5,
        out_specs=(vmem, vmem, vmem),
        scratch_shapes=[pltpu.VMEM(table.shape, table.dtype) for table in tables]
        + [
            pltpu.VMEM((devs * rows_in, LANES), f32),
            pltpu.VMEM((devs, rows_in, LANES), bf16),
            pltpu.VMEM((devs, rows_in, LANES), bf16),
            pltpu.VMEM((devs * max(rows_out, rows_taps), LANES), f32),
            pltpu.VMEM((devs, rows_out, LANES), bf16),
            pltpu.VMEM((devs, rows_out, LANES), bf16),
            pltpu.VMEM((devs, rows_taps, LANES), f32),
            pltpu.VMEM((devs, rows_taps, LANES), f32),
            pltpu.SemaphoreType.DMA((5,)),
            pltpu.SemaphoreType.DMA((3,)),
            pltpu.SemaphoreType.DMA((3, devs)),
            pltpu.SemaphoreType.DMA((3, devs)),
        ],
        compiler_params=pltpu.CompilerParams(
            collective_id=0, has_side_effects=True, vmem_limit_bytes=48 * 1024 * 1024
        ),
    )(skip_gain, signal, filter_param, out_grad, *tables)


def solution(mesh):
    devs = mesh.shape["seq"] * mesh.shape["dp"]
    rows = P(("seq", "dp"), None)
    return jax.shard_map(
        functools.partial(per_device, devs, mesh.shape["dp"]),
        mesh=mesh,
        in_specs=(rows, rows, P(), rows),
        out_specs=(rows, rows, rows),
        check_vma=False,
    )
```

time: 179 us -> 44.4 us (0.25)
  the two profiles are of different devices: /device:TPU:0 before, /device:TPU:25 now
where the time goes in v1:
time: 44.4 us; the launch traced here: 44.1 us
  Pallas kernels  33.5 us (75%)
  local copies, waits for them, and re-layouts  9.95 us (22%)
  between operations  0.66 us (1%)
    pallas_call x1, Pallas kernels, per_device(): pl.pallas_call(functools.partial(kernel, devs, inner_devs, 1.0 / math.sqr...  33.5 us
    unnamed x21, local copies, waits for them, and re-layouts  9.95 us

profile of v1, /device:TPU:25, one launch (start us, length us, event | category | flops | bytes accessed | tf_op | source)
XLA Modules:
  0.0 44.1 jit_solution(1176888842272387820)
XLA Ops:
  0.6 0.0 copy-start
  0.6 0.9 %copy-done = bf16[2,256,256]{2,1,0:T(8,128)(2,1)S(1)} copy-done((bf16[2,256,256]{2,1,0:T(8,128)(2,1)S(1)}, bf16[2,256,256]{2,1,0:T(8,128)(2,1)}, u32[]{:S(2)}) %copy-start) | copy-done | bytes 262168
  1.6 0.0 copy-start.1
  1.6 0.9 %copy-done.1 = bf16[2,256,256]{2,1,0:T(8,128)(2,1)S(1)} copy-done((bf16[2,256,256]{2,1,0:T(8,128)(2,1)S(1)}, bf16[2,256,256]{2,1,0:T(8,128)(2,1)}, u32[]{:S(2)}) %copy-start.1) | copy-done | bytes 262168
  2.5 0.0 copy-start.2
  2.5 0.9 %copy-done.2 = bf16[512,128]{1,0:T(8,128)(2,1)S(1)} copy-done((bf16[512,128]{1,0:T(8,128)(2,1)S(1)}, bf16[512,128]{1,0:T(8,128)(2,1)}, u32[]{:S(2)}) %copy-start.2) | copy-done | bytes 131096
  3.4 0.0 copy-start.3
  3.4 0.9 %copy-done.3 = bf16[512,128]{1,0:T(8,128)(2,1)S(1)} copy-done((bf16[512,128]{1,0:T(8,128)(2,1)S(1)}, bf16[512,128]{1,0:T(8,128)(2,1)}, u32[]{:S(2)}) %copy-start.3) | copy-done | bytes 131096
  4.3 0.0 copy-start.4
  4.3 0.9 %copy-done.4 = bf16[512,128]{1,0:T(8,128)(2,1)S(1)} copy-done((bf16[512,128]{1,0:T(8,128)(2,1)S(1)}, bf16[512,128]{1,0:T(8,128)(2,1)}, u32[]{:S(2)}) %copy-start.4) | copy-done | bytes 131096
  5.2 0.0 copy-start.5
  5.3 0.9 %copy-done.5 = bf16[128,480]{1,0:T(8,128)(2,1)S(1)} copy-done((bf16[128,480]{1,0:T(8,128)(2,1)S(1)}, bf16[128,480]{1,0:T(8,128)(2,1)}, u32[]{:S(2)}) %copy-start.5) | copy-done | bytes 122904
  6.2 0.0 copy-start.6
  6.2 0.9 %copy-done.6 = f32[2,80,128]{2,1,0:T(8,128)S(1)} copy-done((f32[2,80,128]{2,1,0:T(8,128)S(1)}, f32[2,80,128]{2,1,0:T(8,128)}, u32[]{:S(2)}) %copy-start.6) | copy-done | bytes 81944
  7.0 0.0 copy-start.7
  7.0 0.9 %copy-done.7 = bf16[160,256]{1,0:T(8,128)(2,1)S(1)} copy-done((bf16[160,256]{1,0:T(8,128)(2,1)S(1)}, bf16[160,256]{1,0:T(8,128)(2,1)}, u32[]{:S(2)}) %copy-start.7) | copy-done | bytes 81944
  7.9 0.0 copy-start.8
  7.9 0.7 %copy-done.8 = f32[128]{0:T(128)S(1)} copy-done((f32[128]{0:T(128)S(1)}, f32[128]{0:T(128)}, u32[]{:S(2)}) %copy-start.8) | copy-done | bytes 536
  8.6 33.5 %shard_map.112 = (bf16[512,128]{1,0:T(8,128)(2,1)S(1)}, bf16[512,128]{1,0:T(8,128)(2,1)S(1)}, f32[512,128]{1,0:T(8,128)S(1)}) custom-call(f32[128]{0:T(128)S(1)} %copy-done.8, bf16[512,128]{1,0:T(8,128)(2,1)S(1)} %copy-done.2, bf16[512,128]{1,0:T(8,128)(2,1)S(1)} %copy-done.3, bf16[512,128]{1,0:T(8,128)(2,1)S(1)} %copy-done.4, ...), custom_call_target="tpu_custom_call" | custom-call | tf_op jit(solution)/shard_map/pallas_call | solution.py:253
  42.1 0.7 %copy.15 = bf16[512,128]{1,0:T(8,128)(2,1)} copy(bf16[512,128]{1,0:T(8,128)(2,1)S(1)} %get-tuple-element.6) | data formatting | bytes 262144
  42.7 0.7 %copy.16 = bf16[512,128]{1,0:T(8,128)(2,1)} copy(bf16[512,128]{1,0:T(8,128)(2,1)S(1)} %get-tuple-element.7) | data formatting | bytes 262144
  43.4 0.7 %copy.17 = f32[512,128]{1,0:T(8,128)} copy(f32[512,128]{1,0:T(8,128)S(1)} %get-tuple-element.8) | data formatting | bytes 524288
Async XLA Ops:
  0.6 1.0 %copy-start = (bf16[2,256,256]{2,1,0:T(8,128)(2,1)S(1)}, bf16[2,256,256]{2,1,0:T(8,128)(2,1)}, u32[]{:S(2)}) copy-start(bf16[2,256,256]{2,1,0:T(8,128)(2,1)} %constant.13.clone.right_inv_hbm) | copy-start | bytes 786436
  1.6 0.9 %copy-start.1 = (bf16[2,256,256]{2,1,0:T(8,128)(2,1)S(1)}, bf16[2,256,256]{2,1,0:T(8,128)(2,1)}, u32[]{:S(2)}) copy-start(bf16[2,256,256]{2,1,0:T(8,128)(2,1)} %constant.12.clone.right_hbm) | copy-start | bytes 786436
  2.5 0.9 %copy-start.2 = (bf16[512,128]{1,0:T(8,128)(2,1)S(1)}, bf16[512,128]{1,0:T(8,128)(2,1)}, u32[]{:S(2)}) copy-start(bf16[512,128]{1,0:T(8,128)(2,1)} %sig_ref.1) | copy-start | bytes 393220
  3.4 0.9 %copy-start.3 = (bf16[512,128]{1,0:T(8,128)(2,1)S(1)}, bf16[512,128]{1,0:T(8,128)(2,1)}, u32[]{:S(2)}) copy-start(bf16[512,128]{1,0:T(8,128)(2,1)} %filt_ref.1) | copy-start | bytes 393220
  4.3 0.9 %copy-start.4 = (bf16[512,128]{1,0:T(8,128)(2,1)S(1)}, bf16[512,128]{1,0:T(8,128)(2,1)}, u32[]{:S(2)}) copy-start(bf16[512,128]{1,0:T(8,128)(2,1)} %cot_ref.1) | copy-start | bytes 393220
  5.2 0.9 %copy-start.5 = (bf16[128,480]{1,0:T(8,128)(2,1)S(1)}, bf16[128,480]{1,0:T(8,128)(2,1)}, u32[]{:S(2)}) copy-start(bf16[128,480]{1,0:T(8,128)(2,1)} %constant.14.clone.left_inv_hbm) | copy-start | bytes 368644
  6.2 0.9 %copy-start.6 = (f32[2,80,128]{2,1,0:T(8,128)S(1)}, f32[2,80,128]{2,1,0:T(8,128)}, u32[]{:S(2)}) copy-start(f32[2,80,128]{2,1,0:T(8,128)} %constant.11.clone.twiddle_hbm) | copy-start | bytes 245764
  7.0 0.9 %copy-start.7 = (bf16[160,256]{1,0:T(8,128)(2,1)S(1)}, bf16[160,256]{1,0:T(8,128)(2,1)}, u32[]{:S(2)}) copy-start(bf16[160,256]{1,0:T(8,128)(2,1)} %constant.10.clone.left_hbm) | copy-start | bytes 245764
  7.9 0.7 %copy-start.8 = (f32[128]{0:T(128)S(1)}, f32[128]{0:T(128)}, u32[]{:S(2)}) copy-start(f32[128]{0:T(128)} %gain_ref.1) | copy-start | bytes 1540

commit v2 on v1

v2 whole, which is shorter than its diff:
```python
import functools
import math

import jax
import jax.numpy as jnp
import ml_dtypes
import numpy as np
from jax import lax
from jax.experimental import pallas as pl
from jax.experimental.pallas import tpu as pltpu
from jax.sharding import PartitionSpec as P

LANES = 128
MESH = pl.DeviceIdType.MESH


def round_up(value, step):
    return -(-value // step) * step


def split_table(table):
    high = table.astype(np.float32).astype(ml_dtypes.bfloat16)
    low = (table - high.astype(np.float64)).astype(np.float32).astype(ml_dtypes.bfloat16)
    return high, low


def make_tables(length, sources):
    outer = length // LANES
    runs = outer // sources
    half = round_up(outer // 2 + 1, 16)
    k1 = np.arange(half)
    a = (np.arange(sources)[None, :] * runs + np.arange(runs)[:, None]).reshape(-1)
    kept = (k1 <= outer // 2).astype(np.float64)
    angle = 2.0 * math.pi * ((k1[:, None] * a[None, :]) % outer) / outer
    left = np.concatenate([np.cos(angle) * kept[:, None], -np.sin(angle) * kept[:, None]], axis=0)
    left = np.concatenate(split_table(left), axis=1)
    b = np.arange(LANES)
    turn = 2.0 * math.pi * ((k1[:, None] * b[None, :]) % length) / length
    twiddle = np.stack([np.cos(turn), -np.sin(turn)]).astype(np.float32)
    inner = 2.0 * math.pi * ((b[:, None] * b[None, :]) % LANES) / LANES
    cos, sin = np.cos(inner), np.sin(inner)
    right = np.stack(split_table(np.block([[cos, -sin], [sin, cos]])))
    right_inv = np.stack(split_table(np.block([[cos, sin], [-sin, cos]])))
    weight = kept * np.where((k1 == 0) | (2 * k1 == outer), 1.0, 2.0) / length
    left_inv = np.concatenate([np.cos(angle) * weight[:, None], -np.sin(angle) * weight[:, None]], axis=0).T
    high, low = split_table(left_inv)
    left_inv = np.concatenate([high, high, low], axis=1)
    return left, twiddle, right, right_inv, left_inv


def split(value):
    high = value.astype(jnp.bfloat16)
    low = (value - high.astype(jnp.float32)).astype(jnp.bfloat16)
    return high, low


def dot(a, b):
    return jnp.dot(a, b, preferred_element_type=jnp.float32)


def right_product(value, table_ref):
    high, low = split(value)
    return dot(high, table_ref[0]) + dot(low, table_ref[0]) + dot(high, table_ref[1])


def kernel(
    devs, inner_devs, scale,
    gain_ref, sig_hbm, cot_hbm, filt_hbm,
    left_hbm, twiddle_hbm, right_hbm, right_inv_hbm, left_inv_hbm,
    conv_ref, back_ref, taps_ref,
    sig_ref, cot_ref, filt_ref,
    left_ref, twiddle_ref, right_ref, right_inv_ref, left_inv_ref,
    wide_pair, wide_filt, wide_out,
    send_pair, send_filt, send_taps, send_conv, send_back,
    recv_pair, recv_filt, recv_taps, recv_conv, recv_back,
    load_sem, own_sem, send_sem, recv_sem,
):
    rows, chans = sig_ref.shape
    runs = rows // LANES
    mine = chans // devs
    half = twiddle_ref.shape[1]
    me = lax.axis_index("seq") * inner_devs + lax.axis_index("dp")

    def place(index):
        return (index // inner_devs, lax.rem(index, inner_devs))

    loads = [
        pltpu.make_async_copy(src, dst, load_sem.at[at])
        for at, (src, dst) in enumerate(
            [
                (sig_hbm, sig_ref),
                (cot_hbm, cot_ref),
                (filt_hbm, filt_ref),
                (left_hbm, left_ref),
                (twiddle_hbm, twiddle_ref),
                (right_hbm, right_ref),
                (right_inv_hbm, right_inv_ref),
                (left_inv_hbm, left_inv_ref),
            ]
        )
    ]
    for copy in loads:
        copy.start()

    barrier = pltpu.get_barrier_semaphore()

    def greet(step, carry):
        pl.semaphore_signal(barrier, inc=1, device_id=place(lax.rem(me + step, devs)), device_id_type=MESH)
        return carry

    lax.fori_loop(1, devs, greet, 0)

    def exchange(kind, send, recv):
        own = pltpu.make_async_copy(send.at[me], recv.at[me], own_sem.at[kind])
        own.start()

        def remote(to, slot_from, slot_send):
            return pltpu.make_async_remote_copy(
                src_ref=send.at[to],
                dst_ref=recv.at[slot_from],
                send_sem=send_sem.at[kind, slot_send],
                recv_sem=recv_sem.at[kind, slot_from],
                device_id=place(to),
                device_id_type=MESH,
            )

        def begin(step, carry):
            to = lax.rem(me + step, devs)
            remote(to, me, to).start()
            return carry

        lax.fori_loop(1, devs, begin, 0)

        def finish():
            own.wait()

            def arrive(step, carry):
                other = lax.rem(me + devs - step, devs)
                remote(other, other, other).wait_recv()
                return carry

            lax.fori_loop(1, devs, arrive, 0)

        def drain():
            def leave(step, carry):
                to = lax.rem(me + step, devs)
                remote(to, me, to).wait_send()
                return carry

            lax.fori_loop(1, devs, leave, 0)

        return finish, drain

    def pack(ref, at, wide, stride):
        for run in range(runs):
            block = ref[run * LANES : (run + 1) * LANES, :].astype(jnp.float32).T
            for c in range(mine):
                wide[pl.ds((at * mine + c) * runs + run, devs, stride=stride), :] = block[c * devs : (c + 1) * devs, :]

    def narrow(wide, send):
        send[...] = wide[0 : devs * send.shape[1], :].astype(send.dtype).reshape(send.shape)

    def widen(recv, wide):
        wide[0 : devs * recv.shape[1], :] = recv[...].astype(jnp.float32).reshape(devs * recv.shape[1], LANES)

    rows_pair, rows_filt = send_pair.shape[1], send_filt.shape[1]
    loads[0].wait()
    pack(sig_ref, 0, wide_pair, rows_pair)
    loads[1].wait()
    pack(cot_ref, 1, wide_pair, rows_pair)
    narrow(wide_pair, send_pair)
    pl.semaphore_wait(barrier, devs - 1)
    finish_pair, drain_pair = exchange(0, send_pair, recv_pair)
    loads[2].wait()
    pack(filt_ref, 0, wide_filt, rows_filt)
    narrow(wide_filt, send_filt)
    finish_filt, drain_filt = exchange(1, send_filt, recv_filt)
    for copy in loads[3:]:
        copy.wait()

    tw_re, tw_im = twiddle_ref[0], twiddle_ref[1]

    def columns_of(wide, at, stride):
        return [
            jnp.concatenate(
                [wide[pl.ds((at * mine + c) * runs + run, devs, stride=stride), :] for run in range(runs)], axis=0
            )
            for c in range(mine)
        ]

    def forward(columns):
        flat = jnp.concatenate(columns, axis=1).astype(jnp.bfloat16)
        partial = dot(left_ref[...], jnp.concatenate([flat, flat], axis=0))
        turned = []
        for c in range(mine):
            re = partial[:half, c * LANES : (c + 1) * LANES]
            im = partial[half:, c * LANES : (c + 1) * LANES]
            turned.append(jnp.concatenate([re * tw_re - im * tw_im, re * tw_im + im * tw_re], axis=1))
        spec = right_product(jnp.concatenate(turned, axis=0), right_ref)
        return spec[:, :LANES], spec[:, LANES:]

    def inverse(re, im):
        unit = right_product(jnp.concatenate([re, im], axis=1), right_inv_ref)
        turned = []
        for c in range(mine):
            u_re = unit[c * half : (c + 1) * half, :LANES]
            u_im = unit[c * half : (c + 1) * half, LANES:]
            turned.append(jnp.concatenate([u_re * tw_re + u_im * tw_im, u_im * tw_re - u_re * tw_im], axis=0))
        high, low = split(jnp.concatenate(turned, axis=1))
        return dot(left_inv_ref[...], jnp.concatenate([high, low, high], axis=0))

    def unpack(values, send):
        stride = send.shape[1]
        for c in range(mine):
            for run in range(runs):
                wide_out[pl.ds(c * runs + run, devs, stride=stride), :] = values[c][run * devs : (run + 1) * devs, :]
        narrow(wide_out, send)

    def lanes_of(value):
        return [value[:, c * LANES : (c + 1) * LANES] for c in range(mine)]

    finish_pair()
    widen(recv_pair, wide_pair)
    sig_cols = columns_of(wide_pair, 0, rows_pair)
    cot_cols = columns_of(wide_pair, 1, rows_pair)
    sig_re, sig_im = forward(sig_cols)
    cot_re, cot_im = forward(cot_cols)
    taps = inverse(sig_re * cot_re + sig_im * cot_im, sig_re * cot_im - sig_im * cot_re) * scale
    unpack(lanes_of(taps), send_taps)
    finish_taps, drain_taps = exchange(2, send_taps, recv_taps)

    gains = [gain_ref[c * devs + me] for c in range(mine)]
    finish_filt()
    widen(recv_filt, wide_filt)
    filt_re, filt_im = forward(columns_of(wide_filt, 0, rows_filt))
    filt_re, filt_im = filt_re * scale, filt_im * scale
    conv = lanes_of(inverse(sig_re * filt_re - sig_im * filt_im, sig_re * filt_im + sig_im * filt_re))
    unpack([conv[c] + gains[c] * sig_cols[c] for c in range(mine)], send_conv)
    finish_conv, drain_conv = exchange(3, send_conv, recv_conv)
    back = lanes_of(inverse(filt_re * cot_re + filt_im * cot_im, filt_re * cot_im - filt_im * cot_re))
    unpack([back[c] + gains[c] * cot_cols[c] for c in range(mine)], send_back)
    finish_back, drain_back = exchange(4, send_back, recv_back)

    def deliver(recv, out_ref):
        widen(recv, wide_filt)
        stride = recv.shape[1]
        for run in range(runs):
            block = jnp.concatenate(
                [wide_filt[pl.ds(c * runs + run, devs, stride=stride), :] for c in range(mine)], axis=0
            )
            out_ref[run * LANES : (run + 1) * LANES, :] = block.T.astype(out_ref.dtype)

    drain_pair()
    drain_filt()
    finish_taps()
    deliver(recv_taps, taps_ref)
    finish_conv()
    deliver(recv_conv, conv_ref)
    finish_back()
    deliver(recv_back, back_ref)
    drain_taps()
    drain_conv()
    drain_back()


def per_device(devs, inner_devs, signal, filter_param, skip_gain, out_grad):
    rows, chans = signal.shape
    length = rows * devs
    mine = chans // devs
    runs = rows // LANES
    rows_pair = round_up(2 * mine * runs, 16)
    rows_one = round_up(mine * runs, 16)
    rows_taps = round_up(mine * runs, 8)
    tables = [jnp.asarray(table) for table in make_tables(length, devs)]
    bf16, f32 = jnp.bfloat16, jnp.float32
    vmem = pl.BlockSpec(memory_space=pltpu.VMEM)
    hbm = pl.BlockSpec(memory_space=pltpu.HBM)
    slots = [
        pltpu.VMEM((devs, rows_pair, LANES), bf16),
        pltpu.VMEM((devs, rows_one, LANES), bf16),
        pltpu.VMEM((devs, rows_taps, LANES), f32),
        pltpu.VMEM((devs, rows_one, LANES), bf16),
        pltpu.VMEM((devs, rows_one, LANES), bf16),
    ]
    return pl.pallas_call(
        functools.partial(kernel, devs, inner_devs, 1.0 / math.sqrt(length)),
        out_shape=(
            jax.ShapeDtypeStruct((rows, chans), bf16),
            jax.ShapeDtypeStruct((rows, chans), bf16),
            jax.ShapeDtypeStruct((rows, chans), f32),
        ),
        in_specs=[pl.BlockSpec(memory_space=pltpu.SMEM)] + [hbm] * 8,
        out_specs=(vmem, vmem, vmem),
        scratch_shapes=[pltpu.VMEM((rows, chans), bf16)] * 3
        + [pltpu.VMEM(table.shape, table.dtype) for table in tables]
        + [
            pltpu.VMEM((devs * rows_pair, LANES), f32),
            pltpu.VMEM((devs * rows_one, LANES), f32),
            pltpu.VMEM((devs * rows_one, LANES), f32),
        ]
        + slots
        + slots
        + [
            pltpu.SemaphoreType.DMA((8,)),
            pltpu.SemaphoreType.DMA((5,)),
            pltpu.SemaphoreType.DMA((5, devs)),
            pltpu.SemaphoreType.DMA((5, devs)),
        ],
        compiler_params=pltpu.CompilerParams(
            collective_id=0, has_side_effects=True, vmem_limit_bytes=64 * 1024 * 1024
        ),
    )(skip_gain, signal, out_grad, filter_param, *tables)


def solution(mesh):
    devs = mesh.shape["seq"] * mesh.shape["dp"]
    rows = P(("seq", "dp"), None)
    return jax.shard_map(
        functools.partial(per_device, devs, mesh.shape["dp"]),
        mesh=mesh,
        in_specs=(rows, rows, P(), rows),
        out_specs=(rows, rows, rows),
        check_vma=False,
    )
```

time: 44.4 us -> 39.3 us (0.89)
  the two profiles are of different devices: /device:TPU:25 before, /device:TPU:0 now
where the time goes in v2:
time: 39.3 us; the launch traced here: 39.2 us
  Pallas kernels  35.5 us (90%)
  local copies, waits for them, and re-layouts  2.98 us (8%)
  between operations  0.66 us (2%)
    pallas_call x1, Pallas kernels, per_device(): pl.pallas_call(functools.partial(kernel, devs, inner_devs, 1.0 / math.sqr...  35.5 us
    unnamed x7, local copies, waits for them, and re-layouts  2.98 us

profile of v2, /device:TPU:0, one launch (start us, length us, event | category | flops | bytes accessed | tf_op | source)
XLA Modules:
  0.0 39.2 jit_solution(15451180145576523637)
XLA Ops:
  0.6 35.5 %shard_map.112 = (bf16[512,128]{1,0:T(8,128)(2,1)}, bf16[512,128]{1,0:T(8,128)(2,1)}, f32[512,128]{1,0:T(8,128)}) custom-call(f32[128]{0:T(128)} %gain_ref.1, bf16[512,128]{1,0:T(8,128)(2,1)} %sig_hbm.1, bf16[512,128]{1,0:T(8,128)(2,1)} %cot_hbm.1, bf16[512,128]{1,0:T(8,128)(2,1)} %filt_hbm.1, bf16[160,256]{1,0:T(8,128)(2,1)} %constant.10.clone.left_hbm, ...), custom_call_target="tpu_custom_call" | custom-call | tf_op jit(solution)/shard_map/pallas_call | solution.py:285
  36.1 0.0 copy-start.1
  36.2 0.0 copy-start
  36.2 1.6 %copy.15 = bf16[512,128]{1,0:T(8,128)(2,1)} copy(bf16[512,128]{1,0:T(8,128)(2,1)} %get-tuple-element.6) | data formatting | bytes 262144
  37.8 0.0 copy-done.1
  37.8 0.7 %copy.16 = bf16[512,128]{1,0:T(8,128)(2,1)} copy(bf16[512,128]{1,0:T(8,128)(2,1)S(1)} %copy-done.1) | data formatting | bytes 262144
  38.4 0.0 copy-done
  38.4 0.7 %copy.17 = f32[512,128]{1,0:T(8,128)} copy(f32[512,128]{1,0:T(8,128)S(1)} %copy-done) | data formatting | bytes 524288
Async XLA Ops:
  36.1 1.6 %copy-start.1 = (bf16[512,128]{1,0:T(8,128)(2,1)S(1)}, bf16[512,128]{1,0:T(8,128)(2,1)}, u32[]{:S(2)}) copy-start(bf16[512,128]{1,0:T(8,128)(2,1)} %get-tuple-element.7) | copy-start | bytes 393220
  36.2 2.3 %copy-start = (f32[512,128]{1,0:T(8,128)S(1)}, f32[512,128]{1,0:T(8,128)}, u32[]{:S(2)}) copy-start(f32[512,128]{1,0:T(8,128)} %get-tuple-element.8) | copy-start | bytes 786436

commit v3 on v2

--- a/solution.py
+++ b/solution.py
@@ -71,8 +71,8 @@
     sig_ref, cot_ref, filt_ref,
     left_ref, twiddle_ref, right_ref, right_inv_ref, left_inv_ref,
     wide_pair, wide_filt, wide_out,
-    send_pair, send_filt, send_taps, send_conv, send_back,
-    recv_pair, recv_filt, recv_taps, recv_conv, recv_back,
+    send_pair, send_filt, send_taps, send_both,
+    recv_pair, recv_filt, recv_taps, recv_both,
     load_sem, own_sem, send_sem, recv_sem,
 ):
     rows, chans = sig_ref.shape
@@ -114,42 +114,30 @@
         own = pltpu.make_async_copy(send.at[me], recv.at[me], own_sem.at[kind])
         own.start()
 
-        def remote(to, slot_from, slot_send):
+        def remote(to, src, dst):
             return pltpu.make_async_remote_copy(
-                src_ref=send.at[to],
-                dst_ref=recv.at[slot_from],
-                send_sem=send_sem.at[kind, slot_send],
-                recv_sem=recv_sem.at[kind, slot_from],
+                src_ref=src,
+                dst_ref=dst,
+                send_sem=send_sem.at[kind],
+                recv_sem=recv_sem.at[kind],
                 device_id=place(to),
                 device_id_type=MESH,
             )
 
         def begin(step, carry):
             to = lax.rem(me + step, devs)
-            remote(to, me, to).start()
+            remote(to, send.at[to], recv.at[me]).start()
             return carry
 
         lax.fori_loop(1, devs, begin, 0)
+        others = pl.ds(0, devs - 1)
+        all_of_them = remote(lax.rem(me + 1, devs), send.at[others], recv.at[others])
 
         def finish():
             own.wait()
-
-            def arrive(step, carry):
-                other = lax.rem(me + devs - step, devs)
-                remote(other, other, other).wait_recv()
-                return carry
-
-            lax.fori_loop(1, devs, arrive, 0)
-
-        def drain():
-            def leave(step, carry):
-                to = lax.rem(me + step, devs)
-                remote(to, me, to).wait_send()
-                return carry
-
-            lax.fori_loop(1, devs, leave, 0)
-
-        return finish, drain
+            all_of_them.wait_recv()
+
+        return finish, all_of_them.wait_send
 
     def pack(ref, at, wide, stride):
         for run in range(runs):
@@ -209,12 +197,13 @@
         high, low = split(jnp.concatenate(turned, axis=1))
         return dot(left_inv_ref[...], jnp.concatenate([high, low, high], axis=0))
 
-    def unpack(values, send):
+    def unpack(values, send, first=0, last=True):
         stride = send.shape[1]
         for c in range(mine):
             for run in range(runs):
-                wide_out[pl.ds(c * runs + run, devs, stride=stride), :] = values[c][run * devs : (run + 1) * devs, :]
-        narrow(wide_out, send)
+                wide_out[pl.ds((first * mine + c) * runs + run, devs, stride=stride), :] = values[c][run * devs : (run + 1) * devs, :]
+        if last:
+            narrow(wide_out, send)
 
     def lanes_of(value):
         return [value[:, c * LANES : (c + 1) * LANES] for c in range(mine)]
@@ -235,18 +224,18 @@
     filt_re, filt_im = forward(columns_of(wide_filt, 0, rows_filt))
     filt_re, filt_im = filt_re * scale, filt_im * scale
     conv = lanes_of(inverse(sig_re * filt_re - sig_im * filt_im, sig_re * filt_im + sig_im * filt_re))
-    unpack([conv[c] + gains[c] * sig_cols[c] for c in range(mine)], send_conv)
-    finish_conv, drain_conv = exchange(3, send_conv, recv_conv)
+    unpack([conv[c] + gains[c] * sig_cols[c] for c in range(mine)], send_both, 0, False)
     back = lanes_of(inverse(filt_re * cot_re + filt_im * cot_im, filt_re * cot_im - filt_im * cot_re))
-    unpack([back[c] + gains[c] * cot_cols[c] for c in range(mine)], send_back)
-    finish_back, drain_back = exchange(4, send_back, recv_back)
-
-    def deliver(recv, out_ref):
-        widen(recv, wide_filt)
+    unpack([back[c] + gains[c] * cot_cols[c] for c in range(mine)], send_both, 1)
+    finish_both, drain_both = exchange(3, send_both, recv_both)
+
+    def deliver(recv, out_ref, first=0):
+        if first == 0:
+            widen(recv, wide_filt)
         stride = recv.shape[1]
         for run in range(runs):
             block = jnp.concatenate(
-                [wide_filt[pl.ds(c * runs + run, devs, stride=stride), :] for c in range(mine)], axis=0
+                [wide_filt[pl.ds((first * mine + c) * runs + run, devs, stride=stride), :] for c in range(mine)], axis=0
             )
             out_ref[run * LANES : (run + 1) * LANES, :] = block.T.astype(out_ref.dtype)
 
@@ -254,13 +243,11 @@
     drain_filt()
     finish_taps()
     deliver(recv_taps, taps_ref)
-    finish_conv()
-    deliver(recv_conv, conv_ref)
-    finish_back()
-    deliver(recv_back, back_ref)
+    finish_both()
+    deliver(recv_both, conv_ref)
+    deliver(recv_both, back_ref, 1)
     drain_taps()
-    drain_conv()
-    drain_back()
+    drain_both()
 
 
 def per_device(devs, inner_devs, signal, filter_param, skip_gain, out_grad):
@@ -279,8 +266,7 @@
         pltpu.VMEM((devs, rows_pair, LANES), bf16),
         pltpu.VMEM((devs, rows_one, LANES), bf16),
         pltpu.VMEM((devs, rows_taps, LANES), f32),
-        pltpu.VMEM((devs, rows_one, LANES), bf16),
-        pltpu.VMEM((devs, rows_one, LANES), bf16),
+        pltpu.VMEM((devs, rows_pair, LANES), bf16),
     ]
     return pl.pallas_call(
         functools.partial(kernel, devs, inner_devs, 1.0 / math.sqrt(length)),
@@ -295,16 +281,16 @@
         + [pltpu.VMEM(table.shape, table.dtype) for table in tables]
         + [
             pltpu.VMEM((devs * rows_pair, LANES), f32),
-            pltpu.VMEM((devs * rows_one, LANES), f32),
-            pltpu.VMEM((devs * rows_one, LANES), f32),
+            pltpu.VMEM((devs * rows_pair, LANES), f32),
+            pltpu.VMEM((devs * rows_pair, LANES), f32),
         ]
         + slots
         + slots
         + [
             pltpu.SemaphoreType.DMA((8,)),
-            pltpu.SemaphoreType.DMA((5,)),
-            pltpu.SemaphoreType.DMA((5, devs)),
-            pltpu.SemaphoreType.DMA((5, devs)),
+            pltpu.SemaphoreType.DMA((4,)),
+            pltpu.SemaphoreType.DMA((4,)),
+            pltpu.SemaphoreType.DMA((4,)),
         ],
         compiler_params=pltpu.CompilerParams(
             collective_id=0, has_side_effects=True, vmem_limit_bytes=64 * 1024 * 1024

time: 39.3 us -> 34.3 us (0.87)
  the two profiles are of different devices: /device:TPU:0 before, /device:TPU:25 now
where the time goes in v3:
time: 34.3 us; the launch traced here: 34.2 us
  Pallas kernels  30.5 us (89%)
  local copies, waits for them, and re-layouts  2.98 us (9%)
  between operations  0.66 us (2%)
    pallas_call x1, Pallas kernels, per_device(): pl.pallas_call(functools.partial(kernel, devs, inner_devs, 1.0 / math.sqr...  30.5 us
    unnamed x7, local copies, waits for them, and re-layouts  2.98 us

profile of v3, /device:TPU:25, one launch (start us, length us, event | category | flops | bytes accessed | tf_op | source)
XLA Modules:
  0.0 34.2 jit_solution(12150998351757672402)
XLA Ops:
  0.6 30.5 %shard_map.112 = (bf16[512,128]{1,0:T(8,128)(2,1)}, bf16[512,128]{1,0:T(8,128)(2,1)}, f32[512,128]{1,0:T(8,128)}) custom-call(f32[128]{0:T(128)} %gain_ref.1, bf16[512,128]{1,0:T(8,128)(2,1)} %sig_hbm.1, bf16[512,128]{1,0:T(8,128)(2,1)} %cot_hbm.1, bf16[512,128]{1,0:T(8,128)(2,1)} %filt_hbm.1, bf16[160,256]{1,0:T(8,128)(2,1)} %constant.10.clone.left_hbm, ...), custom_call_target="tpu_custom_call" | custom-call | tf_op jit(solution)/shard_map/pallas_call | solution.py:271
  31.2 0.0 copy-start.1
  31.2 0.0 copy-start
  31.2 1.6 %copy.15 = bf16[512,128]{1,0:T(8,128)(2,1)} copy(bf16[512,128]{1,0:T(8,128)(2,1)} %get-tuple-element.6) | data formatting | bytes 262144
  32.8 0.0 copy-done.1
  32.8 0.7 %copy.16 = bf16[512,128]{1,0:T(8,128)(2,1)} copy(bf16[512,128]{1,0:T(8,128)(2,1)S(1)} %copy-done.1) | data formatting | bytes 262144
  33.5 0.0 copy-done
  33.5 0.7 %copy.17 = f32[512,128]{1,0:T(8,128)} copy(f32[512,128]{1,0:T(8,128)S(1)} %copy-done) | data formatting | bytes 524288
Async XLA Ops:
  31.2 1.6 %copy-start.1 = (bf16[512,128]{1,0:T(8,128)(2,1)S(1)}, bf16[512,128]{1,0:T(8,128)(2,1)}, u32[]{:S(2)}) copy-start(bf16[512,128]{1,0:T(8,128)(2,1)} %get-tuple-element.7) | copy-start | bytes 393220
  31.2 2.3 %copy-start = (f32[512,128]{1,0:T(8,128)S(1)}, f32[512,128]{1,0:T(8,128)}, u32[]{:S(2)}) copy-start(f32[512,128]{1,0:T(8,128)} %get-tuple-element.8) | copy-start | bytes 786436

commit v4 on v3

--- a/solution.py
+++ b/solution.py
@@ -58,13 +58,24 @@
     return jnp.dot(a, b, preferred_element_type=jnp.float32)
 
 
+def encode(value, shift):
+    value = value * shift
+    square = value * value
+    return jnp.where(value < 0.0, -square * square, square * square)
+
+
+def decode(code, shift):
+    root = jnp.sqrt(jnp.sqrt(jnp.abs(code))) * (1.0 / shift)
+    return jnp.where(code < 0.0, -root, root)
+
+
 def right_product(value, table_ref):
     high, low = split(value)
     return dot(high, table_ref[0]) + dot(low, table_ref[0]) + dot(high, table_ref[1])
 
 
 def kernel(
-    devs, inner_devs, scale,
+    devs, inner_devs, scale, shift,
     gain_ref, sig_hbm, cot_hbm, filt_hbm,
     left_hbm, twiddle_hbm, right_hbm, right_inv_hbm, left_inv_hbm,
     conv_ref, back_ref, taps_ref,
@@ -215,7 +226,7 @@
     sig_re, sig_im = forward(sig_cols)
     cot_re, cot_im = forward(cot_cols)
     taps = inverse(sig_re * cot_re + sig_im * cot_im, sig_re * cot_im - sig_im * cot_re) * scale
-    unpack(lanes_of(taps), send_taps)
+    unpack(lanes_of(encode(taps, shift)), send_taps)
     finish_taps, drain_taps = exchange(2, send_taps, recv_taps)
 
     gains = [gain_ref[c * devs + me] for c in range(mine)]
@@ -229,7 +240,7 @@
     unpack([back[c] + gains[c] * cot_cols[c] for c in range(mine)], send_both, 1)
     finish_both, drain_both = exchange(3, send_both, recv_both)
 
-    def deliver(recv, out_ref, first=0):
+    def deliver(recv, out_ref, first=0, shift=None):
         if first == 0:
             widen(recv, wide_filt)
         stride = recv.shape[1]
@@ -237,17 +248,29 @@
             block = jnp.concatenate(
                 [wide_filt[pl.ds((first * mine + c) * runs + run, devs, stride=stride), :] for c in range(mine)], axis=0
             )
+            block = block if shift is None else decode(block, shift)
             out_ref[run * LANES : (run + 1) * LANES, :] = block.T.astype(out_ref.dtype)
 
     drain_pair()
     drain_filt()
     finish_taps()
-    deliver(recv_taps, taps_ref)
+    deliver(recv_taps, taps_ref, shift=shift)
     finish_both()
     deliver(recv_both, conv_ref)
     deliver(recv_both, back_ref, 1)
     drain_taps()
     drain_both()
+
+
+def hand_over(conv_ref, back_ref, taps_ref, conv_out, back_out, taps_out, sem):
+    copies = [
+        pltpu.make_async_copy(src, dst, sem.at[at])
+        for at, (src, dst) in enumerate(((conv_ref, conv_out), (back_ref, back_out), (taps_ref, taps_out)))
+    ]
+    for copy in copies:
+        copy.start()
+    for copy in copies:
+        copy.wait()
 
 
 def per_device(devs, inner_devs, signal, filter_param, skip_gain, out_grad):
@@ -257,7 +280,7 @@
     runs = rows // LANES
     rows_pair = round_up(2 * mine * runs, 16)
     rows_one = round_up(mine * runs, 16)
-    rows_taps = round_up(mine * runs, 8)
+    shift = 2.0 ** (31 - math.ceil(math.log2(36.0 * math.sqrt(length))))
     tables = [jnp.asarray(table) for table in make_tables(length, devs)]
     bf16, f32 = jnp.bfloat16, jnp.float32
     vmem = pl.BlockSpec(memory_space=pltpu.VMEM)
@@ -265,16 +288,17 @@
     slots = [
         pltpu.VMEM((devs, rows_pair, LANES), bf16),
         pltpu.VMEM((devs, rows_one, LANES), bf16),
-        pltpu.VMEM((devs, rows_taps, LANES), f32),
+        pltpu.VMEM((devs, rows_one, LANES), bf16),
         pltpu.VMEM((devs, rows_pair, LANES), bf16),
     ]
-    return pl.pallas_call(
-        functools.partial(kernel, devs, inner_devs, 1.0 / math.sqrt(length)),
-        out_shape=(
-            jax.ShapeDtypeStruct((rows, chans), bf16),
-            jax.ShapeDtypeStruct((rows, chans), bf16),
-            jax.ShapeDtypeStruct((rows, chans), f32),
-        ),
+    shapes = (
+        jax.ShapeDtypeStruct((rows, chans), bf16),
+        jax.ShapeDtypeStruct((rows, chans), bf16),
+        jax.ShapeDtypeStruct((rows, chans), f32),
+    )
+    made = pl.pallas_call(
+        functools.partial(kernel, devs, inner_devs, 1.0 / math.sqrt(length), shift),
+        out_shape=shapes,
         in_specs=[pl.BlockSpec(memory_space=pltpu.SMEM)] + [hbm] * 8,
         out_specs=(vmem, vmem, vmem),
         scratch_shapes=[pltpu.VMEM((rows, chans), bf16)] * 3
@@ -296,6 +320,14 @@
             collective_id=0, has_side_effects=True, vmem_limit_bytes=64 * 1024 * 1024
         ),
     )(skip_gain, signal, out_grad, filter_param, *tables)
+    place = pl.BlockSpec(memory_space=pl.ANY)
+    return pl.pallas_call(
+        hand_over,
+        out_shape=shapes,
+        in_specs=[vmem] * 3,
+        out_specs=[place] * 3,
+        scratch_shapes=[pltpu.SemaphoreType.DMA((3,))],
+    )(*made)
 
 
 def solution(mesh):

time: 34.3 us -> 31 us (0.904)
  the two profiles are of different devices: /device:TPU:25 before, /device:TPU:0 now
where the time goes in v4:
time: 31 us; the launch traced here: 30.6 us
  Pallas kernels  29.9 us (96%)
  between operations  0.64 us (2%)
    pallas_call x1, Pallas kernels, per_device(): pl.pallas_call(functools.partial(kernel, devs, inner_devs, 1.0 / math.sqr...  28 us
    pallas_call x1, Pallas kernels, per_device(): pl.pallas_call(hand_over, out_shape=shapes, in_specs=[vmem] * 3, out_spec...  1.9 us

profile of v4, /device:TPU:0, one launch (start us, length us, event | category | flops | bytes accessed | tf_op | source)
XLA Modules:
  0.0 30.6 jit_solution(1629794867223164830)
XLA Ops:
  0.6 28.0 %shard_map.112 = (bf16[512,128]{1,0:T(8,128)(2,1)}, bf16[512,128]{1,0:T(8,128)(2,1)}, f32[512,128]{1,0:T(8,128)}) custom-call(f32[128]{0:T(128)} %gain_ref.1, bf16[512,128]{1,0:T(8,128)(2,1)} %sig_hbm.1, bf16[512,128]{1,0:T(8,128)(2,1)} %cot_hbm.1, bf16[512,128]{1,0:T(8,128)(2,1)} %filt_hbm.1, bf16[160,256]{1,0:T(8,128)(2,1)} %constant.10.clone.left_hbm, ...), custom_call_target="tpu_custom_call" | custom-call | tf_op jit(solution)/shard_map/pallas_call | solution.py:299
  28.7 1.9 %shard_map.113 = (bf16[512,128]{1,0:T(8,128)(2,1)}, bf16[512,128]{1,0:T(8,128)(2,1)}, f32[512,128]{1,0:T(8,128)}) custom-call(bf16[512,128]{1,0:T(8,128)(2,1)} %get-tuple-element.6.conv_ref, bf16[512,128]{1,0:T(8,128)(2,1)} %get-tuple-element.7.back_ref, f32[512,128]{1,0:T(8,128)} %get-tuple-element.8.taps_ref), custom_call_target="tpu_custom_call" | custom-call | tf_op jit(solution)/shard_map/pallas_call | solution.py:324

commit v5 on v4

--- a/solution.py
+++ b/solution.py
@@ -76,15 +76,16 @@
 
 def kernel(
     devs, inner_devs, scale, shift,
-    gain_ref, sig_hbm, cot_hbm, filt_hbm,
+    gain_hbm, sig_hbm, cot_hbm, filt_hbm,
     left_hbm, twiddle_hbm, right_hbm, right_inv_hbm, left_inv_hbm,
+    conv_hbm, back_hbm, taps_hbm,
     conv_ref, back_ref, taps_ref,
     sig_ref, cot_ref, filt_ref,
     left_ref, twiddle_ref, right_ref, right_inv_ref, left_inv_ref,
     wide_pair, wide_filt, wide_out,
     send_pair, send_filt, send_taps, send_both,
     recv_pair, recv_filt, recv_taps, recv_both,
-    load_sem, own_sem, send_sem, recv_sem,
+    gain_ref, load_sem, own_sem, send_sem, recv_sem, store_sem,
 ):
     rows, chans = sig_ref.shape
     runs = rows // LANES
@@ -107,6 +108,7 @@
                 (right_hbm, right_ref),
                 (right_inv_hbm, right_inv_ref),
                 (left_inv_hbm, left_inv_ref),
+                (gain_hbm, gain_ref),
             ]
         )
     ]
@@ -251,15 +253,24 @@
             block = block if shift is None else decode(block, shift)
             out_ref[run * LANES : (run + 1) * LANES, :] = block.T.astype(out_ref.dtype)
 
+    stores = [
+        pltpu.make_async_copy(src, dst, store_sem.at[at])
+        for at, (src, dst) in enumerate(((taps_ref, taps_hbm), (conv_ref, conv_hbm), (back_ref, back_hbm)))
+    ]
     drain_pair()
     drain_filt()
     finish_taps()
     deliver(recv_taps, taps_ref, shift=shift)
+    stores[0].start()
     finish_both()
     deliver(recv_both, conv_ref)
+    stores[1].start()
     deliver(recv_both, back_ref, 1)
+    stores[2].start()
     drain_taps()
     drain_both()
+    for copy in stores:
+        copy.wait()
 
 
 def hand_over(conv_ref, back_ref, taps_ref, conv_out, back_out, taps_out, sem):
@@ -299,9 +310,10 @@
     made = pl.pallas_call(
         functools.partial(kernel, devs, inner_devs, 1.0 / math.sqrt(length), shift),
         out_shape=shapes,
-        in_specs=[pl.BlockSpec(memory_space=pltpu.SMEM)] + [hbm] * 8,
-        out_specs=(vmem, vmem, vmem),
-        scratch_shapes=[pltpu.VMEM((rows, chans), bf16)] * 3
+        in_specs=[hbm] * 9,
+        out_specs=(hbm, hbm, hbm),
+        scratch_shapes=[pltpu.VMEM(shape.shape, shape.dtype) for shape in shapes]
+        + [pltpu.VMEM((rows, chans), bf16)] * 3
         + [pltpu.VMEM(table.shape, table.dtype) for table in tables]
         + [
             pltpu.VMEM((devs * rows_pair, LANES), f32),
@@ -311,10 +323,12 @@
         + slots
         + slots
         + [
-            pltpu.SemaphoreType.DMA((8,)),
+            pltpu.SMEM((chans,), f32),
+            pltpu.SemaphoreType.DMA((9,)),
             pltpu.SemaphoreType.DMA((4,)),
             pltpu.SemaphoreType.DMA((4,)),
             pltpu.SemaphoreType.DMA((4,)),
+            pltpu.SemaphoreType.DMA((3,)),
         ],
         compiler_params=pltpu.CompilerParams(
             collective_id=0, has_side_effects=True, vmem_limit_bytes=64 * 1024 * 1024

time: 31 us -> 30.2 us (0.974)
  Pallas kernels: 29.9 us -> 29.2 us
    pallas_call x1, Pallas kernels: 28 us -> 27.3 us  [per_device(): pl.pallas_call(functools.partial(kernel, devs, inner_devs, 1.0 / math.sqr...]
where the time goes in v5:
time: 30.2 us; the launch traced here: 29.8 us
  Pallas kernels  29.2 us (97%)
  between operations  0.64 us (2%)
    pallas_call x1, Pallas kernels, per_device(): pl.pallas_call(functools.partial(kernel, devs, inner_devs, 1.0 / math.sqr...  27.3 us
    pallas_call x1, Pallas kernels, per_device(): pl.pallas_call(hand_over, out_shape=shapes, in_specs=[vmem] * 3, out_spec...  1.9 us

profile of v5, /device:TPU:0, one launch (start us, length us, event | category | flops | bytes accessed | tf_op | source)
XLA Modules:
  0.0 29.8 jit_solution(5835170218080783978)
XLA Ops:
  0.6 27.3 %shard_map.112 = (bf16[512,128]{1,0:T(8,128)(2,1)}, bf16[512,128]{1,0:T(8,128)(2,1)}, f32[512,128]{1,0:T(8,128)}) custom-call(f32[128]{0:T(128)} %gain_hbm.1, bf16[512,128]{1,0:T(8,128)(2,1)} %sig_hbm.1, bf16[512,128]{1,0:T(8,128)(2,1)} %cot_hbm.1, bf16[512,128]{1,0:T(8,128)(2,1)} %filt_hbm.1, bf16[160,256]{1,0:T(8,128)(2,1)} %constant.10.clone.left_hbm, ...), custom_call_target="tpu_custom_call" | custom-call | tf_op jit(solution)/shard_map/pallas_call | solution.py:310
  27.9 1.9 %shard_map.113 = (bf16[512,128]{1,0:T(8,128)(2,1)}, bf16[512,128]{1,0:T(8,128)(2,1)}, f32[512,128]{1,0:T(8,128)}) custom-call(bf16[512,128]{1,0:T(8,128)(2,1)} %get-tuple-element.6.conv_ref, bf16[512,128]{1,0:T(8,128)(2,1)} %get-tuple-element.7.back_ref, f32[512,128]{1,0:T(8,128)} %get-tuple-element.8.taps_ref), custom_call_target="tpu_custom_call" | custom-call | tf_op jit(solution)/shard_map/pallas_call | solution.py:338
